TPU v7x, 32 devices: a whole 2x2x4 slice. The times are simulated.
32 devices in a mesh: blk: 8 (over y, x, core), group: 4 (over z).
Axes of the slice: x: 2, y: 2, z: 4, core: 2. Of those that a mesh axis runs over, the one named last changes fastest.
Arguments:
- centres: bfloat16 [65536, 1024], P(('blk', 'group')), may hold values from -8 to 8
- batch_x: bfloat16 [512, 1024], P(('blk', 'group')), may hold values from -8 to 8
- grad: bfloat16 [512, 1000], P(('blk', 'group')), may hold values from -0.29882812 to 0.29882812
- eigvec: float32 [16384, 128], P(('blk', 'group')), may hold values from -0.046875 to 0.046875
- eig_scale: float32 [128], replicated, may hold values from 2 to 20
- sub_index: int32 [16384], P(('blk', 'group')), may hold values from 0 to 65535, as said below
Outputs:
- update: float32 [65536, 1000], P(('blk', 'group'))
Inputs may be any that keep to these rules, and one draw needn't show every extreme that they name: `sub_index`: all entries are distinct. Entry i of the block of 512 entries that device index k of blk+group holds names a centre among rows (k // 4) * 4 * 2048 to (k // 4 + 1) * 4 * 2048 - 1; among one such block at most 128 entries name rows of any one aligned run of 2048 centres, and every block has exactly 128 in one run.
All inputs are finite; a program needn't handle non-finite values.
Results may differ from a plain program's by a relative error of at most 0.0027.
Values may be sent and summed in bfloat16 or wider, within the bound.
A program may use at most 128 MiB of HBM per device.

v0:
```python
import jax
import jax.numpy as jnp
from jax import lax
from jax.sharding import PartitionSpec as P

D = 1024
CAP = 128


def body(centres, batch_x, grad, eigvec, eig_scale, sub_index):
    centre_sq = jnp.sum(jnp.square(centres.astype(jnp.float32)), axis=1)
    piece_x = lax.all_gather(batch_x, ("blk", "group"), axis=0, tiled=True)
    piece_g = lax.all_gather(grad, ("blk", "group"), axis=0, tiled=True)
    batch_sq = jnp.sum(jnp.square(piece_x.astype(jnp.float32)), axis=1)
    inner_prod = jnp.einsum("cd,bd->cb", centres, piece_x, preferred_element_type=jnp.float32)
    distance = centre_sq[:, None] + batch_sq[None, :] - 2.0 * inner_prod
    kernel_tile = jnp.exp(-distance / (2.0 * D)).astype(jnp.bfloat16)
    kernel_grad = jnp.dot(kernel_tile, piece_g, preferred_element_type=jnp.float32)
    groups = lax.axis_size("group")
    rows_each = centres.shape[0]
    classes = grad.shape[1]
    holder = sub_index // rows_each % groups
    local_row = sub_index % rows_each
    onehot = (holder[:, None] == jnp.arange(groups, dtype=jnp.int32)[None, :]).astype(jnp.int32)
    order_in = jnp.sum(jnp.cumsum(onehot, axis=0) * onehot, axis=1) - 1
    position = holder * CAP + order_in
    slot_table = (
        jnp.zeros((groups * CAP,), jnp.int32).at[position].set(local_row).reshape(groups, CAP)
    )
    got_slots = lax.all_to_all(slot_table, "group", split_axis=0, concat_axis=0, tiled=True)
    flat_slots = got_slots.reshape(-1)
    fetched_rows = kernel_grad[flat_slots].reshape(groups, CAP, classes)
    returned = lax.all_to_all(fetched_rows, "group", split_axis=0, concat_axis=0, tiled=True)
    picked = returned.reshape(groups * CAP, classes)[position]
    projected = lax.psum(
        jnp.einsum("sq,sk->qk", eigvec, picked, precision=lax.Precision.HIGHEST), ("blk", "group")
    )
    correction = jnp.dot(eigvec * eig_scale[None, :], projected, precision=lax.Precision.HIGHEST)
    correction_table = jnp.zeros((groups * CAP, classes), jnp.float32).at[position].set(correction)
    correction_table = correction_table.reshape(groups, CAP, classes)
    got_correction = lax.all_to_all(
        correction_table, "group", split_axis=0, concat_axis=0, tiled=True
    )
    return kernel_grad.at[flat_slots].add(-got_correction.reshape(groups * CAP, classes))


def solution(mesh):
    in_specs = (
        P(("blk", "group"), None),
        P(("blk", "group"), None),
        P(("blk", "group"), None),
        P(("blk", "group"), None),
        P(),
        P(("blk", "group")),
    )
    out_specs = P(("blk", "group"), None)
    return jax.shard_map(body, mesh=mesh, in_specs=in_specs, out_specs=out_specs, check_vma=False)
```

profile of v0, /device:TPU:0, one launch (start us, length us, event | category | flops | bytes accessed | tf_op | source)
XLA Modules:
  0.0 394.1 jit_solution(16455057887739230425)
XLA Ops:
  6.5 0.0 all-gather.2.cloned.1.call-start
  6.5 0.7 all-gather.2.cloned.1.call-update
  7.3 0.7 add_select_fusion
  8.0 1.2 reduce-window.6
  9.2 0.2 slice_reduce_fusion
  9.4 0.2 reduce-window.9
  9.6 0.1 add_bitcast_fusion
  9.7 3.0 scatter_custom_fusion
  12.7 6.3 %all-to-all-start = ((s32[4,1,128]{2,1,0:T(1,128)}), s32[4,1,128]{2,1,0:T(1,128)S(1)}, u32[]{:S(2)}, u32[]{:S(2)}) async-start(s32[4,1,128]{2,1,0:T(1,128)} %bitcast.2), calls=%async_computation | async-start | bytes 4096 | tf_op jit(solution)/shard_map/all_to_all | solution.py:30
  19.0 78.8 %all_gather.7 = bf16[512,1000]{1,0:T(8,128)(2,1)S(1)} all-gather(bf16[16,1000]{1,0:T(8,128)(2,1)} %param.8), channel_id=1, replica_groups=mesh['blk'=8,'group'=4] {'blk','group'}, dimensions={0}, use_global_device_ids=true | all-gather | bytes 1056000 | tf_op jit(solution)/shard_map/all_gather | solution.py:13
  97.8 3.1 multiply_reduce_fusion
  100.9 0.0 all-to-all-done
  100.9 0.0 all-gather.2.cloned.1.call-done
  101.0 1.5 multiply_reduce_fusion.1
  102.5 10.7 %fusion.2 = f32[2048,1000]{1,0:T(8,128)} fusion(bf16[512,1000]{1,0:T(8,128)(2,1)S(1)} %all_gather.7, bf16[2048,1024]{1,0:T(8,128)(2,1)} %param.6, bf16[512,1024]{1,0:T(8,128)(2,1)} %all-gather.2.cloned.1.call-done, f32[512]{0:T(512)S(1)} %multiply_reduce_fusion.1, f32[2048]{0:T(1024)S(1)} %multiply_reduce_fusion), kind=kOutput, calls=%fused_computation.11 | convolution fusion | flops 4250927104 | bytes 14469120 | tf_op jit(solution)/shard_map/dot_general | solution.py:18
  113.2 6.2 %gather_fusion = f32[512,1000]{1,0:T(8,128)S(1)} fusion(f32[2048,1000]{1,0:T(8,128)} %fusion.2, s32[1024]{0:T(1024)S(1)} %pad_clamp_fusion.1), kind=kCustom, calls=%fused_computation | custom fusion | bytes 4098048 | tf_op jit(solution)/shard_map/gather | solution.py:32
  119.4 1.8 copy.20
  121.2 4.5 %all-to-all-start.1 = ((f32[4,128,1000]{1,2,0:T(8,128)}), f32[4,128,1000]{1,2,0:T(8,128)}, u32[]{:S(2)}, u32[]{:S(2)}) async-start(f32[4,128,1000]{1,2,0:T(8,128)} %copy.20), calls=%async_computation.1 | async-start | bytes 4096000 | tf_op jit(solution)/shard_map/all_to_all | solution.py:33
  125.7 0.2 all-reduce.2.cloned.1.call-start
  125.9 41.9 %all-to-all-done.1 = f32[4,128,1000]{1,2,0:T(8,128)} async-done(((f32[4,128,1000]{1,2,0:T(8,128)}), f32[4,128,1000]{1,2,0:T(8,128)}, u32[]{:S(2)}, u32[]{:S(2)}) %all-to-all-start.1) | async-done | bytes 2048032 | tf_op jit(solution)/shard_map/all_to_all | solution.py:33
  167.9 1.9 copy.21
  169.8 0.0 copy-start
  169.8 2.7 gather_fusion.1
  172.4 0.0 copy-done
  172.4 0.0 copy-start.1
  172.5 5.9 %convolution_bitcast_fusion = f32[128,1000]{0,1:T(8,128)} fusion(f32[512,1000]{1,0:T(8,128)} %gather_fusion.1, f32[512,128]{1,0:T(8,128)S(1)} %copy-done), kind=kOutput, calls=%fused_computation.8 | convolution fusion | flops 786432000 | bytes 2822144 | tf_op jit(solution)/shard_map/sq,sk->qk/dot_general | solution.py:36
  178.4 0.0 all-reduce.2.cloned.1.call-update
  178.4 125.1 %all-reduce.2.cloned.1.call-done = f32[128,1000]{0,1:T(8,128)} async-done(((f32[128,1000]{0,1:T(8,128)}), f32[128,1000]{0,1:T(8,128)}) %all-reduce.2.cloned.1.call-update) | async-done | bytes 512016 | tf_op jit(solution)/shard_map/psum | solution.py:35
  303.5 0.0 copy-done.1
  303.5 4.2 %fusion.3 = f32[512,1000]{1,0:T(8,128)} fusion(f32[128,1000]{0,1:T(8,128)} %all-reduce.2.cloned.1.call-done, f32[512,128]{1,0:T(8,128)S(1)} %copy-done, f32[128]{0:T(128)S(1)} %copy-done.1), kind=kOutput, calls=%fused_computation.12 | convolution fusion | flops 786497536 | bytes 2822656 | tf_op jit(solution)/shard_map/dot_general | solution.py:38
  307.6 3.8 scatter_custom_fusion.1
  311.4 1.8 copy.23
  313.2 50.3 %all_to_all.19 = f32[4,128,1000]{1,2,0:T(8,128)S(1)} all-to-all(f32[4,128,1000]{1,2,0:T(8,128)} %copy.23), channel_id=1, replica_groups=mesh['blk'=8,'group'=4] {'group'}, dimensions={0} | all-to-all | bytes 4096000 | tf_op jit(solution)/shard_map/all_to_all | solution.py:41
  363.5 1.4 neg.10
  365.0 1.9 copy.24
  366.9 11.2 %scatter_fusion = f32[2048,1000]{1,0:T(8,128)} fusion(f32[2048,1000]{1,0:T(8,128)} %fusion.2, s32[512]{0:T(512)S(1)} %bitcast.40, f32[512,1000]{1,0:T(8,128)S(1)} %bitcast.35), kind=kCustom, calls=%fused_computation.4 | custom fusion | flops 512000 | bytes 6146048 | tf_op jit(solution)/shard_map/scatter-add | solution.py:44
  378.1 9.1 %copy.26 = f32[2048,1000]{0,1:T(8,128)} copy(f32[2048,1000]{1,0:T(8,128)} %scatter_fusion) | data formatting | bytes 16384000 | tf_op jit(solution)/shard_map/scatter-add | solution.py:44
  (6 shorter events, 0.1 us)
Async XLA Ops:
  6.5 94.4 %all-gather.2.cloned.1.call-start = ((), (), s32[]{:S(2)}) async-start(), calls=%async_computation.3 | async-start | bytes 1081344 | tf_op jit(solution)/shard_map/all_gather | solution.py:12
  12.7 88.2 %all-to-all-start = ((s32[4,1,128]{2,1,0:T(1,128)}), s32[4,1,128]{2,1,0:T(1,128)S(1)}, u32[]{:S(2)}, u32[]{:S(2)}) async-start(s32[4,1,128]{2,1,0:T(1,128)} %bitcast.2), calls=%async_computation | async-start | bytes 4096 | tf_op jit(solution)/shard_map/all_to_all | solution.py:30
  121.2 46.7 %all-to-all-start.1 = ((f32[4,128,1000]{1,2,0:T(8,128)}), f32[4,128,1000]{1,2,0:T(8,128)}, u32[]{:S(2)}, u32[]{:S(2)}) async-start(f32[4,128,1000]{1,2,0:T(8,128)} %copy.20), calls=%async_computation.1 | async-start | bytes 4096000 | tf_op jit(solution)/shard_map/all_to_all | solution.py:33
  125.7 177.8 %all-reduce.2.cloned.1.call-start = ((), (), s32[]{:S(2)}) async-start(), calls=%async_computation.4 | async-start | bytes 1024000 | tf_op jit(solution)/shard_map/psum | solution.py:35
  169.8 2.7 copy-start
  172.4 131.0 %copy-start.1 = (f32[128]{0:T(128)S(1)}, f32[128]{0:T(128)}, u32[]{:S(2)}) copy-start(f32[128]{0:T(128)} %param.10) | copy-start | bytes 1540
Sparse Core Ops, SparseCore 0:
  10.3 56.8 all-gather.1
  178.5 124.9 all-reduce.1
where the time goes:
time: 395 us; the launch traced here: 394 us
  waiting for transfers between devices  168 us (43%)
  blocking collectives  129 us (33%)
  local copies, waits for them, and re-layouts  32.4 us (8%)
  matrix products  20.8 us (5%)
  other arithmetic  19.5 us (5%)
  between operations  13.5 us (3%)
  starting transfers between devices  11 us (3%)
    psum x1, waiting for transfers between devices, body(): lax.psum(jnp.einsum('sq,sk->qk', eigvec, picked, precision=lax.Precision....  125 us
    all_gather x1, blocking collectives, body(): piece_g = lax.all_gather(grad, ('blk', 'group'), axis=0, tiled=True)  78.8 us
    all_to_all x1, blocking collectives, body(): lax.all_to_all(correction_table, 'group', split_axis=0, concat_axis=0, ti...  50.3 us
    all_to_all x1, waiting for transfers between devices, body(): lax.all_to_all(fetched_rows, 'group', split_axis=0, concat_axis=0, tiled=...  41.9 us
    scatter-add x1, other arithmetic, body(): kernel_grad.at[flat_slots]  11.2 us
    dot_general x1, matrix products, body(): jnp.dot(kernel_tile, piece_g, preferred_element_type=jnp.float32)  10.7 us
    scatter-add x1, local copies, waits for them, and re-layouts, body(): kernel_grad.at[flat_slots]  9.15 us
  transfers between devices with their start and end apart: 4, of which 2 were waited for; matrix products, arithmetic and copies ran while one was open for 2% of the time, Pallas kernels for 0%

commit v1 on v0

v1 whole, which is shorter than its diff:
```python
import functools

import jax
import jax.numpy as jnp
from jax import lax
from jax.experimental import pallas as pl
from jax.experimental.pallas import tpu as pltpu
from jax.sharding import PartitionSpec as P

CAP = 128
TILE = 256
F32, BF16 = jnp.float32, jnp.bfloat16


def nt(a, b):
    return lax.dot_general(a, b, (((1,), (1,)), ((), ())), preferred_element_type=F32)


def split(a):
    hi = a.astype(BF16)
    return hi, (a - hi.astype(F32)).astype(BF16)


def onehot(a, b):
    return jnp.where(a == b, 1.0, 0.0).astype(BF16)


def copy_to(src, dst, send, recv, blk, grp):
    return pltpu.make_async_remote_copy(
        src_ref=src,
        dst_ref=dst,
        send_sem=send,
        recv_sem=recv,
        device_id=(blk, grp),
        device_id_type=pl.DeviceIdType.MESH,
    )


class Gather:
    def __init__(self, me, grid, own, whole, send, recv):
        self.me, self.grid, self.own, self.whole, self.send, self.recv = me, grid, own, whole, send, recv
        self.sent = []

    def push(self, src, slot, blk, grp):
        copy = copy_to(src, self.whole.at[slot], self.send.at[len(self.sent)], self.recv.at[slot], blk, grp)
        copy.start()
        self.sent.append(copy)

    def wait(self, slot):
        blk, grp = self.me
        there = self.whole.at[slot]
        copy_to(there, there, self.send.at[0], self.recv.at[slot], self.twin, grp).wait_recv()

    @property
    def twin(self):
        blk, _ = self.me
        return blk + 1 - 2 * lax.rem(blk, 2)

    def chips(self):
        blk, _ = self.me
        n = self.grid[0] // 2
        core, chip = lax.rem(blk, 2), lax.div(blk, 2)
        return [2 * lax.rem(chip + k, n) + core for k in range(1, n)]

    def groups(self):
        _, grp = self.me
        return [lax.rem(grp + k, self.grid[1]) for k in range(1, self.grid[1])]

    def slot(self, blk, grp):
        return blk * self.grid[1] + grp

    def first(self):
        blk, grp = self.me
        slot = self.slot(blk, grp)
        self.whole[slot] = self.own[...]
        for other in self.groups():
            self.push(self.own, slot, blk, other)
        for other in self.chips():
            self.push(self.own, slot, other, grp)
        self.push(self.own, slot, self.twin, grp)

    def second(self):
        blk, grp = self.me
        for source in self.groups():
            slot = self.slot(blk, source)
            self.wait(slot)
            for other in self.chips():
                self.push(self.whole.at[slot], slot, other, grp)
            self.push(self.whole.at[slot], slot, self.twin, grp)

    def third(self):
        _, grp = self.me
        for source in [grp] + self.groups():
            for other in self.chips():
                slot = self.slot(other, source)
                self.wait(slot)
                self.push(self.whole.at[slot], slot, self.twin, grp)

    def last(self):
        _, grp = self.me
        n = self.grid[0] // 2
        core = lax.rem(self.twin, 2)
        for chip in range(n):
            for source in range(self.grid[1]):
                self.wait(self.slot(2 * chip + core, source))

    def drain(self):
        for copy in self.sent:
            copy.wait_send()


def exchange(
    grid, x_ref, g_ref, vec_ref, scale_ref, index_ref, c_hbm, gp_ref, rhs_ref,
    xall, gall, cbuf, csq, vec_out, vec_in, row_out, row_in, acc,
    part, part_in, some, some_in, full,
    c_sem, x_send, x_recv, g_send, g_recv, v_send, v_recv, r_send, r_recv,
    p_send, p_recv, s_send, s_recv, f_send, f_recv,
):
    n_blk, n_grp = grid
    blk, grp = lax.axis_index("blk"), lax.axis_index("group")
    n_rows, dim = cbuf.shape
    subs = vec_ref.shape[0]
    q = vec_ref.shape[1]
    batch = xall.shape[0] * xall.shape[1]
    piece = batch // n_blk
    classes = g_ref.shape[1]
    tiles = n_rows // TILE

    load = pltpu.make_async_copy(c_hbm, cbuf, c_sem)
    load.start()

    other_grps = [lax.rem(grp + k, n_grp) for k in range(1, n_grp)]
    other_blks = [lax.rem(blk + k, n_blk) for k in range(1, n_blk)]
    barrier = pltpu.get_barrier_semaphore()
    for other in other_grps:
        pl.semaphore_signal(barrier, inc=1, device_id=(blk, other), device_id_type=pl.DeviceIdType.MESH)
    for other in other_blks:
        pl.semaphore_signal(barrier, inc=1, device_id=(other, grp), device_id_type=pl.DeviceIdType.MESH)
    pl.semaphore_wait(barrier, n_grp + n_blk - 2)

    xs = Gather((blk, grp), grid, x_ref, xall, x_send, x_recv)
    gs = Gather((blk, grp), grid, g_ref, gall, g_send, g_recv)
    xs.first()

    index = jnp.broadcast_to(index_ref[...], (8, subs))
    shift = n_rows.bit_length() - 1
    local = index & (n_rows - 1)
    holder = lax.shift_right_logical(index, shift) & (n_grp - 1)
    line = lax.broadcasted_iota(jnp.int32, (8, subs), 0)
    member = jnp.where(holder == line, 1.0, 0.0)
    upper = jnp.where(
        lax.broadcasted_iota(jnp.int32, (subs, subs), 0) < lax.broadcasted_iota(jnp.int32, (subs, subs), 1), 1.0, 0.0
    ).astype(BF16)
    order = jnp.sum(member * jnp.dot(member.astype(BF16), upper, preferred_element_type=F32), axis=0, keepdims=True)
    position = holder[0:1].astype(F32) * CAP + order
    places = n_grp * CAP
    select = onehot(lax.broadcasted_iota(jnp.int32, (places, subs), 0).astype(F32), position)
    vec_hi, vec_lo = split(vec_ref[...])
    table = jnp.dot(select, jnp.concatenate([vec_hi, vec_lo], axis=1), preferred_element_type=F32).T
    wanted = jnp.where(line == 0, lax.shift_right_logical(local, 7), jnp.where(line == 1, local & 127, 1))
    rows = nt(wanted.astype(F32).astype(BF16), select)
    for k in range(n_grp):
        vec_out[k] = table[:, k * CAP : (k + 1) * CAP].astype(BF16)
        row_out[k] = rows[:, k * CAP : (k + 1) * CAP]
    vecs = []
    for k, other in enumerate(other_grps):
        vecs.append(copy_to(vec_out.at[other], vec_in.at[grp], v_send.at[k], v_recv.at[grp], blk, other))
        vecs.append(copy_to(row_out.at[other], row_in.at[grp], r_send.at[k], r_recv.at[grp], blk, other))
    for copy in vecs:
        copy.start()
    vec_in[grp] = vec_out[grp]
    row_in[grp] = row_out[grp]

    xs.second()
    gs.first()

    load.wait()
    ones = jnp.ones((8, 128), BF16)

    @pl.loop(0, tiles)
    def _(t):
        block = cbuf[pl.ds(pl.multiple_of(t * TILE, TILE), TILE), :].astype(F32)
        square = block * block
        total = square[:, :128]
        for k in range(1, dim // 128):
            total = total + square[:, k * 128 : (k + 1) * 128]
        hi = total.astype(BF16)
        mid, low = split(total - hi.astype(F32))
        csq[:, pl.ds(pl.multiple_of(t * TILE, TILE), TILE)] = nt(ones, hi) + nt(ones, mid) + nt(ones, low)

    xs.third()
    gs.second()

    for other in other_grps:
        copy_to(vec_in.at[other], vec_in.at[other], v_send.at[0], v_recv.at[other], blk, other).wait_recv()
        copy_to(row_in.at[other], row_in.at[other], r_send.at[0], r_recv.at[other], blk, other).wait_recv()
    vec_all = jnp.concatenate([vec_in[k] for k in range(n_grp)], axis=1)
    rows = jnp.concatenate([row_in[k] for k in range(n_grp)], axis=1)
    place = rows[0:1] * 128.0 + rows[1:2] + (rows[2:3] - 1.0) * (2.0 * n_rows)

    @pl.loop(0, tiles)
    def _(t):
        where = (lax.broadcasted_iota(jnp.int32, (TILE, places), 0) + t * TILE).astype(F32)
        at_centres = nt(vec_all, onehot(where, place)).astype(BF16)
        columns = pl.ds(pl.multiple_of(t * TILE, TILE), TILE)
        rhs_ref[batch : batch + 2 * q, columns] = at_centres
        rhs_ref[batch + 2 * q :, columns] = at_centres[:q]

    xs.last()
    x = xall[...].reshape(batch, dim)
    xf = x.astype(F32)
    bsq = jnp.sum(xf * xf, axis=1, keepdims=True)
    acc[...] = jnp.zeros_like(acc)

    @pl.loop(0, tiles)
    def _(t):
        columns = pl.ds(pl.multiple_of(t * TILE, TILE), TILE)
        inner = nt(xall[...].reshape(batch, dim), cbuf[columns, :])
        distance = csq[0:1, columns] + bsq - 2.0 * inner
        kern = jnp.exp(distance * (-0.5 / dim)).astype(BF16)
        rhs_ref[0:batch, columns] = kern
        acc[...] += nt(kern, rhs_ref[batch : batch + 2 * q, columns])

    both = acc[:, :q] + acc[:, q:]
    for k in range(n_blk):
        part[k] = both[k * piece : (k + 1) * piece]
    parts = [
        copy_to(part.at[other], part_in.at[blk], p_send.at[k], p_recv.at[blk], other, grp)
        for k, other in enumerate(other_blks)
    ]
    for copy in parts:
        copy.start()
    part_in[blk] = part[blk]
    gs.third()
    for other in other_blks:
        copy_to(part_in.at[other], part_in.at[other], p_send.at[0], p_recv.at[other], other, grp).wait_recv()
    some[...] = functools.reduce(jnp.add, [part_in[k] for k in range(n_blk)])
    somes = [
        copy_to(some, some_in.at[grp], s_send.at[k], s_recv.at[grp], blk, other) for k, other in enumerate(other_grps)
    ]
    for copy in somes:
        copy.start()
    some_in[grp] = some[...]
    gs.last()
    gp_ref[0:batch] = gall[...].reshape(batch, classes)
    for other in other_grps:
        copy_to(some_in.at[other], some_in.at[other], s_send.at[0], s_recv.at[other], blk, other).wait_recv()
    full[blk] = functools.reduce(jnp.add, [some_in[k] for k in range(n_grp)])
    fulls = [
        copy_to(full.at[blk], full.at[blk], f_send.at[k], f_recv.at[blk], other, grp)
        for k, other in enumerate(other_blks)
    ]
    for copy in fulls:
        copy.start()
    for other in other_blks:
        copy_to(full.at[other], full.at[other], f_send.at[0], f_recv.at[other], other, grp).wait_recv()

    scaled = (full[...].reshape(batch, q) * scale_ref[...]).T
    hi, lo = split(scaled)
    product = jnp.dot(jnp.concatenate([hi, lo], axis=0), gp_ref[0:batch], preferred_element_type=F32)
    hi, lo = split(-(product[:q] + product[q:]))
    gp_ref[batch : batch + q] = hi
    gp_ref[batch + q : batch + 2 * q] = hi
    gp_ref[batch + 2 * q :] = lo

    xs.drain()
    gs.drain()
    for copy in vecs + parts + somes + fulls:
        copy.wait_send()


def body(grid, centres, batch_x, grad, eigvec, eig_scale, sub_index):
    n_blk, n_grp = grid
    n_dev = n_blk * n_grp
    n_rows, dim = centres.shape
    mine, classes = grad.shape
    subs, q = eigvec.shape
    batch = mine * n_dev
    piece = batch // n_blk
    dma = pltpu.SemaphoreType.DMA
    vmem = pl.BlockSpec(memory_space=pltpu.VMEM)
    gp, rhs = pl.pallas_call(
        functools.partial(exchange, grid),
        out_shape=(
            jax.ShapeDtypeStruct((batch + 3 * q, classes), BF16),
            jax.ShapeDtypeStruct((batch + 3 * q, n_rows), BF16),
        ),
        in_specs=[vmem] * 5 + [pl.BlockSpec(memory_space=pl.ANY)],
        out_specs=(vmem, vmem),
        scratch_shapes=[
            pltpu.VMEM((n_dev, mine, dim), BF16),
            pltpu.VMEM((n_dev, mine, classes), BF16),
            pltpu.VMEM((n_rows, dim), BF16),
            pltpu.VMEM((8, n_rows), F32),
            pltpu.VMEM((n_grp, 2 * q, CAP), BF16),
            pltpu.VMEM((n_grp, 2 * q, CAP), BF16),
            pltpu.VMEM((n_grp, 8, CAP), F32),
            pltpu.VMEM((n_grp, 8, CAP), F32),
            pltpu.VMEM((batch, 2 * q), F32),
            pltpu.VMEM((n_blk, piece, q), F32),
            pltpu.VMEM((n_blk, piece, q), F32),
            pltpu.VMEM((piece, q), F32),
            pltpu.VMEM((n_grp, piece, q), F32),
            pltpu.VMEM((n_blk, piece, q), F32),
            dma,
            dma((n_dev,)),
            dma((n_dev,)),
            dma((n_dev,)),
            dma((n_dev,)),
            dma((n_grp,)),
            dma((n_grp,)),
            dma((n_grp,)),
            dma((n_grp,)),
            dma((n_blk,)),
            dma((n_blk,)),
            dma((n_grp,)),
            dma((n_grp,)),
            dma((n_blk,)),
            dma((n_blk,)),
        ],
        compiler_params=pltpu.CompilerParams(
            collective_id=0, has_side_effects=True, vmem_limit_bytes=58 * 2**20
        ),
        cost_estimate=pl.CostEstimate(
            flops=2 * batch * n_rows * (dim + 2 * q), bytes_accessed=2 * n_rows * dim, transcendentals=batch * n_rows
        ),
    )(batch_x, grad, eigvec, eig_scale.reshape(1, q), sub_index.reshape(1, subs), centres)
    out = lax.dot_general(gp, rhs, (((0,), (0,)), ((), ())), preferred_element_type=F32)
    return out.T


def solution(mesh):
    grid = (mesh.shape["blk"], mesh.shape["group"])
    rows = P(("blk", "group"), None)
    in_specs = (rows, rows, rows, rows, P(), P(("blk", "group")))
    return jax.shard_map(
        functools.partial(body, grid), mesh=mesh, in_specs=in_specs, out_specs=rows, check_vma=False
    )
```

time: 395 us -> 54.5 us (0.14)
  waiting for transfers between devices: 168 us -> 0 us
  blocking collectives: 129 us -> 0 us
  Pallas kernels: 0 us -> 44 us
  local copies, waits for them, and re-layouts: 32.4 us -> 0 us
  other arithmetic: 19.5 us -> 0 us
  between operations: 13.5 us -> 0.01 us
  starting transfers between devices: 11 us -> 0 us
  matrix products: 20.8 us -> 10.4 us
    psum x1 -> x0, waiting for transfers between devices: 125 us -> none  [body(): lax.psum(jnp.einsum('sq,sk->qk', eigvec, picked, precision=lax.Precision....]
    all_gather x1 -> x0, blocking collectives: 78.8 us -> none  [body(): piece_g = lax.all_gather(grad, ('blk', 'group'), axis=0, tiled=True)]
    all_to_all x1 -> x0, blocking collectives: 50.3 us -> none  [body(): lax.all_to_all(correction_table, 'group', split_axis=0, concat_axis=0, ti...]
    pallas_call x0 -> x1, Pallas kernels: none -> 44 us  [body(): pl.pallas_call(functools.partial(exchange, grid), out_shape=(jax.ShapeDty...]
    all_to_all x2 -> x0, waiting for transfers between devices: 41.9 us -> none  [the longest x1 41.9 us: body(): lax.all_to_all(fetched_rows, 'group', split_axis=0, concat_axis=0, tiled=...]
    scatter-add x1 -> x0, other arithmetic: 11.2 us -> none  [body(): kernel_grad.at[flat_slots]]
    all_to_all x2 -> x0, starting transfers between devices: 10.8 us -> none  [the longest x1 6.32 us: body(): lax.all_to_all(slot_table, 'group', split_axis=0, concat_axis=0, tiled=True)]
    dot_general x3 -> x1, matrix products: 20.8 us -> 10.4 us  [body(): lax.dot_general(gp, rhs, (((0,), (0,)), ((), ())), preferred_element_type...]
  transfers between devices with their start and end apart: 4 -> 0, of which waited for: 2 -> 0; matrix products, arithmetic and copies ran while one was open for 2% -> 0% of each run, Pallas kernels for 0% -> 0%
where the time goes in v1:
time: 54.5 us; the launch traced here: 54.4 us
  Pallas kernels  44 us (81%)
  matrix products  10.4 us (19%)
    pallas_call x1, Pallas kernels, body(): pl.pallas_call(functools.partial(exchange, grid), out_shape=(jax.ShapeDty...  44 us
    dot_general x1, matrix products, body(): lax.dot_general(gp, rhs, (((0,), (0,)), ((), ())), preferred_element_type...  10.4 us

profile of v1, /device:TPU:0, one launch (start us, length us, event | category | flops | bytes accessed | tf_op | source)
XLA Modules:
  0.0 54.4 jit_solution(18128381420634499435)
XLA Ops:
  0.0 44.0 %shard_map.64 = (bf16[896,1000]{1,0:T(8,128)(2,1)}, bf16[896,2048]{1,0:T(8,128)(2,1)}) custom-call(bf16[16,1024]{1,0:T(8,128)(2,1)} %x_ref.1, bf16[16,1000]{1,0:T(8,128)(2,1)} %g_ref.1, f32[512,128]{1,0:T(8,128)} %vec_ref.1, f32[1,128]{1,0:T(1,128)} %bitcast.5, s32[1,512]{1,0:T(1,128)} %bitcast.4, bf16[2048,1024]{1,0:T(8,128)(2,1)} %c_hbm.1), custom_call_target="tpu_custom_call" | custom-call | flops 2684354560 | bytes 4194304 | tf_op jit(solution)/shard_map/pallas_call | solution.py:282
  44.0 10.4 %fusion = f32[2048,1000]{0,1:T(8,128)} fusion(bf16[896,2048]{1,0:T(8,128)(2,1)} %get-tuple-element.7, bf16[896,1000]{1,0:T(8,128)(2,1)} %get-tuple-element.8), kind=kOutput, calls=%fused_computation | convolution fusion | flops 3670016000 | bytes 13654016 | tf_op jit(solution)/shard_map/dot_general | solution.py:328

commit v2 on v1

--- a/solution.py
+++ b/solution.py
@@ -9,6 +9,7 @@
 
 CAP = 128
 TILE = 256
+WIDE = 1024
 F32, BF16 = jnp.float32, jnp.bfloat16
 
 
@@ -110,10 +111,11 @@
 
 
 def exchange(
-    grid, x_ref, g_ref, vec_ref, scale_ref, index_ref, c_hbm, gp_ref, rhs_ref,
+    grid, x_ref, g_ref, vec_ref, scale_ref, index_ref, c_hbm, gp_hbm, rhs_hbm,
+    gp_ref, rhs_ref,
     xall, gall, cbuf, csq, vec_out, vec_in, row_out, row_in, acc,
-    part, part_in, some, some_in, full,
-    c_sem, x_send, x_recv, g_send, g_recv, v_send, v_recv, r_send, r_recv,
+    part, part_in, some, some_in, full, gown,
+    c_sem, o_sem, x_send, x_recv, g_send, g_recv, v_send, v_recv, r_send, r_recv,
     p_send, p_recv, s_send, s_recv, f_send, f_recv,
 ):
     n_blk, n_grp = grid
@@ -124,10 +126,13 @@
     batch = xall.shape[0] * xall.shape[1]
     piece = batch // n_blk
     classes = g_ref.shape[1]
+    wide = gown.shape[1]
     tiles = n_rows // TILE
 
     load = pltpu.make_async_copy(c_hbm, cbuf, c_sem)
     load.start()
+    gown[...] = jnp.zeros_like(gown)
+    gown[:, :classes] = g_ref[...]
 
     other_grps = [lax.rem(grp + k, n_grp) for k in range(1, n_grp)]
     other_blks = [lax.rem(blk + k, n_blk) for k in range(1, n_blk)]
@@ -139,7 +144,7 @@
     pl.semaphore_wait(barrier, n_grp + n_blk - 2)
 
     xs = Gather((blk, grp), grid, x_ref, xall, x_send, x_recv)
-    gs = Gather((blk, grp), grid, g_ref, gall, g_send, g_recv)
+    gs = Gather((blk, grp), grid, gown, gall, g_send, g_recv)
     xs.first()
 
     index = jnp.broadcast_to(index_ref[...], (8, subs))
@@ -204,7 +209,6 @@
         at_centres = nt(vec_all, onehot(where, place)).astype(BF16)
         columns = pl.ds(pl.multiple_of(t * TILE, TILE), TILE)
         rhs_ref[batch : batch + 2 * q, columns] = at_centres
-        rhs_ref[batch + 2 * q :, columns] = at_centres[:q]
 
     xs.last()
     x = xall[...].reshape(batch, dim)
@@ -212,9 +216,9 @@
     bsq = jnp.sum(xf * xf, axis=1, keepdims=True)
     acc[...] = jnp.zeros_like(acc)
 
-    @pl.loop(0, tiles)
-    def _(t):
-        columns = pl.ds(pl.multiple_of(t * TILE, TILE), TILE)
+    @pl.loop(0, n_rows // WIDE)
+    def _(t):
+        columns = pl.ds(pl.multiple_of(t * WIDE, WIDE), WIDE)
         inner = nt(xall[...].reshape(batch, dim), cbuf[columns, :])
         distance = csq[0:1, columns] + bsq - 2.0 * inner
         kern = jnp.exp(distance * (-0.5 / dim)).astype(BF16)
@@ -231,6 +235,8 @@
     for copy in parts:
         copy.start()
     part_in[blk] = part[blk]
+    right = pltpu.make_async_copy(rhs_ref, rhs_hbm, o_sem.at[0])
+    right.start()
     gs.third()
     for other in other_blks:
         copy_to(part_in.at[other], part_in.at[other], p_send.at[0], p_recv.at[other], other, grp).wait_recv()
@@ -242,10 +248,17 @@
         copy.start()
     some_in[grp] = some[...]
     gs.last()
-    gp_ref[0:batch] = gall[...].reshape(batch, classes)
+
+    @pl.loop(0, wide // TILE)
+    def _(t):
+        columns = pl.ds(pl.multiple_of(t * TILE, TILE), TILE)
+        gp_ref[columns, 0:batch] = gall[:, :, columns].reshape(batch, TILE).astype(F32).T.astype(BF16)
+
+    left = pltpu.make_async_copy(gp_ref.at[:, 0:batch], gp_hbm.at[:, 0:batch], o_sem.at[1])
+    left.start()
     for other in other_grps:
         copy_to(some_in.at[other], some_in.at[other], s_send.at[0], s_recv.at[other], blk, other).wait_recv()
-    full[blk] = functools.reduce(jnp.add, [some_in[k] for k in range(n_grp)])
+    full[blk] = functools.reduce(jnp.add, [some_in[k] for k in range(n_grp)]).astype(BF16)
     fulls = [
         copy_to(full.at[blk], full.at[blk], f_send.at[k], f_recv.at[blk], other, grp)
         for k, other in enumerate(other_blks)
@@ -255,18 +268,55 @@
     for other in other_blks:
         copy_to(full.at[other], full.at[other], f_send.at[0], f_recv.at[other], other, grp).wait_recv()
 
-    scaled = (full[...].reshape(batch, q) * scale_ref[...]).T
-    hi, lo = split(scaled)
-    product = jnp.dot(jnp.concatenate([hi, lo], axis=0), gp_ref[0:batch], preferred_element_type=F32)
-    hi, lo = split(-(product[:q] + product[q:]))
-    gp_ref[batch : batch + q] = hi
-    gp_ref[batch + q : batch + 2 * q] = hi
-    gp_ref[batch + 2 * q :] = lo
-
+    product = jnp.dot(gp_ref[:, 0:batch], full[...].reshape(batch, q), preferred_element_type=F32)
+    hi = (product * -scale_ref[...]).astype(BF16)
+    gp_ref[:, batch : batch + q] = hi
+    gp_ref[:, batch + q : batch + 2 * q] = hi
+
+    rest = pltpu.make_async_copy(gp_ref.at[:, batch:], gp_hbm.at[:, batch:], o_sem.at[2])
+    rest.start()
     xs.drain()
     gs.drain()
     for copy in vecs + parts + somes + fulls:
         copy.wait_send()
+    for copy in (right, left, rest):
+        copy.wait()
+
+
+def final(gp_hbm, rhs_hbm, out_hbm, gp, rhs, out, gp_sem, rhs_sem, out_sem):
+    classes = out.shape[0]
+    tiles = rhs.shape[1] // WIDE
+
+    def left(k):
+        rows = pl.ds(k * TILE, TILE)
+        return pltpu.make_async_copy(gp_hbm.at[rows], gp.at[rows], gp_sem.at[k])
+
+    def column(t):
+        return pl.ds(pl.multiple_of(t * WIDE, WIDE), WIDE)
+
+    def right(t):
+        return pltpu.make_async_copy(rhs_hbm.at[:, column(t)], rhs.at[:, column(t)], rhs_sem.at[t])
+
+    def result(t):
+        return pltpu.make_async_copy(out.at[:, column(t)], out_hbm.at[:, column(t)], out_sem.at[t])
+
+    right(0).start()
+    for k in range(gp.shape[0] // TILE):
+        left(k).start()
+    for t in range(1, tiles):
+        right(t).start()
+    for k in range(gp.shape[0] // TILE):
+        left(k).wait()
+
+    @pl.loop(0, tiles)
+    def _(t):
+        right(t).wait()
+        out[:, column(t)] = jnp.dot(gp[...], rhs[:, column(t)], preferred_element_type=F32)[:classes]
+        result(t).start()
+
+    @pl.loop(0, tiles)
+    def _(t):
+        result(t).wait()
 
 
 def body(grid, centres, batch_x, grad, eigvec, eig_scale, sub_index):
@@ -277,19 +327,24 @@
     subs, q = eigvec.shape
     batch = mine * n_dev
     piece = batch // n_blk
+    wide = pl.cdiv(classes, TILE) * TILE
+    deep = batch + 2 * q
     dma = pltpu.SemaphoreType.DMA
     vmem = pl.BlockSpec(memory_space=pltpu.VMEM)
+    anywhere = pl.BlockSpec(memory_space=pl.ANY)
     gp, rhs = pl.pallas_call(
         functools.partial(exchange, grid),
         out_shape=(
-            jax.ShapeDtypeStruct((batch + 3 * q, classes), BF16),
-            jax.ShapeDtypeStruct((batch + 3 * q, n_rows), BF16),
+            jax.ShapeDtypeStruct((wide, deep), BF16),
+            jax.ShapeDtypeStruct((deep, n_rows), BF16),
         ),
-        in_specs=[vmem] * 5 + [pl.BlockSpec(memory_space=pl.ANY)],
-        out_specs=(vmem, vmem),
+        in_specs=[vmem] * 5 + [anywhere],
+        out_specs=(anywhere, anywhere),
         scratch_shapes=[
+            pltpu.VMEM((wide, deep), BF16),
+            pltpu.VMEM((deep, n_rows), BF16),
             pltpu.VMEM((n_dev, mine, dim), BF16),
-            pltpu.VMEM((n_dev, mine, classes), BF16),
+            pltpu.VMEM((n_dev, mine, wide), BF16),
             pltpu.VMEM((n_rows, dim), BF16),
             pltpu.VMEM((8, n_rows), F32),
             pltpu.VMEM((n_grp, 2 * q, CAP), BF16),
@@ -301,8 +356,10 @@
             pltpu.VMEM((n_blk, piece, q), F32),
             pltpu.VMEM((piece, q), F32),
             pltpu.VMEM((n_grp, piece, q), F32),
-            pltpu.VMEM((n_blk, piece, q), F32),
+            pltpu.VMEM((n_blk, piece, q), BF16),
+            pltpu.VMEM((mine, wide), BF16),
             dma,
+            dma((3,)),
             dma((n_dev,)),
             dma((n_dev,)),
             dma((n_dev,)),
@@ -325,7 +382,24 @@
             flops=2 * batch * n_rows * (dim + 2 * q), bytes_accessed=2 * n_rows * dim, transcendentals=batch * n_rows
         ),
     )(batch_x, grad, eigvec, eig_scale.reshape(1, q), sub_index.reshape(1, subs), centres)
-    out = lax.dot_general(gp, rhs, (((0,), (0,)), ((), ())), preferred_element_type=F32)
+    out = pl.pallas_call(
+        final,
+        out_shape=jax.ShapeDtypeStruct((classes, n_rows), F32),
+        in_specs=[anywhere, anywhere],
+        out_specs=anywhere,
+        scratch_shapes=[
+            pltpu.VMEM((wide, deep), BF16),
+            pltpu.VMEM((deep, n_rows), BF16),
+            pltpu.VMEM((classes, n_rows), F32),
+            dma((wide // TILE,)),
+            dma((n_rows // WIDE,)),
+            dma((n_rows // WIDE,)),
+        ],
+        compiler_params=pltpu.CompilerParams(vmem_limit_bytes=60 * 2**20),
+        cost_estimate=pl.CostEstimate(
+            flops=2 * wide * deep * n_rows, bytes_accessed=4 * classes * n_rows, transcendentals=0
+        ),
+    )(gp, rhs)
     return out.T
 
 

time: 54.5 us -> 47.6 us (0.87)
  matrix products: 10.4 us -> 0 us
  Pallas kernels: 44 us -> 47.5 us
    dot_general x1 -> x0, matrix products: 10.4 us -> none  [body(): lax.dot_general(gp, rhs, (((0,), (0,)), ((), ())), preferred_element_type...]
    pallas_call x0 -> x1, Pallas kernels: none -> 7.46 us  [body(): pl.pallas_call(final, out_shape=jax.ShapeDtypeStruct((classes, n_rows), F...]
    pallas_call x1, Pallas kernels: 44 us -> 40 us  [body(): pl.pallas_call(functools.partial(exchange, grid), out_shape=(jax.ShapeDty...]
where the time goes in v2:
time: 47.6 us; the launch traced here: 47.5 us
  Pallas kernels  47.5 us (100%)
    pallas_call x1, Pallas kernels, body(): pl.pallas_call(functools.partial(exchange, grid), out_shape=(jax.ShapeDty...  40 us
    pallas_call x1, Pallas kernels, body(): pl.pallas_call(final, out_shape=jax.ShapeDtypeStruct((classes, n_rows), F...  7.46 us

profile of v2, /device:TPU:0, one launch (start us, length us, event | category | flops | bytes accessed | tf_op | source)
XLA Modules:
  0.0 47.5 jit_solution(6211357356813739089)
XLA Ops:
  0.0 40.0 %shard_map.64 = (bf16[1024,768]{1,0:T(8,128)(2,1)}, bf16[768,2048]{1,0:T(8,128)(2,1)}) custom-call(bf16[16,1024]{1,0:T(8,128)(2,1)} %x_ref.1, bf16[16,1000]{1,0:T(8,128)(2,1)} %g_ref.1, f32[512,128]{1,0:T(8,128)} %vec_ref.1, f32[1,128]{1,0:T(1,128)} %bitcast.4, s32[1,512]{1,0:T(1,128)} %bitcast.3, bf16[2048,1024]{1,0:T(8,128)(2,1)} %c_hbm.1), custom_call_target="tpu_custom_call" | custom-call | flops 2684354560 | bytes 4194304 | tf_op jit(solution)/shard_map/pallas_call | solution.py:335
  40.0 7.5 %shard_map.65 = f32[1000,2048]{1,0:T(8,128)} custom-call(bf16[1024,768]{1,0:T(8,128)(2,1)} %get-tuple-element.7.gp_hbm, bf16[768,2048]{1,0:T(8,128)(2,1)} %get-tuple-element.8.rhs_hbm), custom_call_target="tpu_custom_call" | custom-call | flops 3221225472 | bytes 8192000 | tf_op jit(solution)/shard_map/pallas_call | solution.py:385
